TPU v7x, 32 devices: a whole 2x2x4 slice. The times are simulated.
32 devices in a mesh: mem: 4 (over y, x), grid: 8 (over z, core).
Axes of the slice: x: 2, y: 2, z: 4, core: 2. Of those that a mesh axis runs over, the one named last changes fastest.
Arguments:
- ens_state: bfloat16 [80, 128, 512], P('mem', 'grid'), may hold values from -6 to 6
- obs_prior: bfloat16 [80, 3072, 128], P('mem', 'grid'), may hold values from -6 to 6
- obs_value: float32 [3072, 128], P('grid'), may hold values from -6 to 6
- obs_prec: float32 [3072, 128], P('grid'), may hold values from 0.01 to 0.2
- obs_len: int32 [3072], P('grid'), may hold values from 1 to 128, as said below
- pair_block: int32 [128, 256], P('grid'), may hold values from 0 to 3071, as said below
- obs_pos: float32 [3072, 128], P('grid'), may hold values from 0 to 128, as said below
Outputs:
- analysis: bfloat16 [80, 128, 512], P('mem', 'grid')
Inputs may be any that keep to these rules, and one draw needn't show every extreme that they name: `obs_len`: count of valid slots of each observation block; slots at or past it are padding. Row b lists 256 distinct observation blocks; for each, pair_block[b,p] // 384 - b // 16 is -1, 0 or 1 modulo 3072 // 384. `obs_pos`: positions along the cyclic band of 128 state blocks.
All inputs are finite; a program needn't handle non-finite values. Where the computation divides by a largest or mean magnitude, that divisor is 1e-20 or more.
Results may differ from a plain program's by a relative error of at most 0.0058.
Values may be sent and summed in bfloat16 or wider, within the bound.
A program may use at most 128 MiB of HBM per device.

v0:
```python
import math

import jax
import jax.numpy as jnp
from jax import lax
from jax.sharding import PartitionSpec as P

NSIT = 3
LOCR = 8


inflation = 1.1


def extended(block, sides, width):
    for axis, dim in sides:
        count = lax.axis_size(axis)
        forward = [(i, i + 1) for i in range(count - 1)]
        forward.append((count - 1, 0))
        backward = [(target, source) for source, target in forward]
        low = lax.ppermute(
            lax.slice_in_dim(block, block.shape[dim] - width, None, axis=dim), axis, forward
        )
        high = lax.ppermute(lax.slice_in_dim(block, 0, width, axis=dim), axis, backward)
        block = jnp.concatenate([low, block, high], axis=dim)
    return block


def finish(gram_matrix, forcing):
    members = gram_matrix.shape[0]
    highest = lax.Precision.HIGHEST
    identity = jnp.eye(members, dtype=jnp.float32)
    system = gram_matrix + (members - 1) / inflation * identity
    bound_sum = jnp.max(jnp.sum(jnp.abs(system), axis=1))
    y_iter = system / bound_sum
    z_iter = identity
    for sweep in range(NSIT):
        factor = 1.5 * identity - 0.5 * jnp.dot(z_iter, y_iter, precision=highest)
        y_iter = jnp.dot(y_iter, factor, precision=highest)
        z_iter = jnp.dot(factor, z_iter, precision=highest)
    root_inv = z_iter / jnp.sqrt(bound_sum)
    mean_weight = jnp.dot(
        root_inv, jnp.dot(root_inv, forcing, precision=highest), precision=highest
    )
    return (math.sqrt(members - 1) * root_inv + mean_weight[:, None]).astype(jnp.bfloat16)


def block_terms(window, aux_window, block_ids, center, nb_total):
    chosen = jnp.take(window, block_ids, axis=1)
    departure = jnp.take(aux_window[0], block_ids, axis=0)
    precision_obs = jnp.take(aux_window[1], block_ids, axis=0)
    position = jnp.take(aux_window[2], block_ids, axis=0)
    distance = jnp.abs(position - center)
    distance = jnp.minimum(distance, nb_total - distance)
    relative = distance / LOCR
    weight = precision_obs * jnp.exp(-0.5 * relative * relative)
    scaled = (chosen.astype(jnp.float32) * weight).astype(jnp.bfloat16)
    gram_matrix = lax.dot_general(
        scaled, chosen, (((1, 2), (1, 2)), ((), ())), preferred_element_type=jnp.float32
    )
    forcing = jnp.einsum(
        "ipk,pk->i", scaled.astype(jnp.float32), departure, precision=lax.Precision.HIGHEST
    )
    return (gram_matrix, forcing)


def run_groups(func, items, count):
    group = math.gcd(count, 2)
    shaped = jax.tree.map(lambda arr: arr.reshape((count // group, group) + arr.shape[1:]), items)
    result = lax.map(lambda part_items: jax.vmap(func)(*part_items), shaped)
    return jax.tree.map(lambda arr: arr.reshape((count,) + arr.shape[2:]), result)


def per_device(ens_state, obs_prior, obs_value, obs_prec, obs_len, pair_block, obs_pos):
    mem_count = lax.axis_size("mem")
    grid_count = lax.axis_size("grid")
    members = mem_count * ens_state.shape[0]
    blocks_dev = ens_state.shape[1]
    obs_blocks = obs_prior.shape[1]
    owned = blocks_dev // mem_count
    obs_sums, state_sums = lax.psum(
        (
            jnp.sum(obs_prior, axis=0, dtype=jnp.float32),
            jnp.sum(ens_state, axis=0, dtype=jnp.float32),
        ),
        "mem",
    )
    obs_mean = obs_sums / members
    state_mean = state_sums / members
    valid = lax.broadcasted_iota(jnp.int32, obs_mean.shape, 1) < obs_len[:, None]
    perturb = jnp.where(valid, obs_prior.astype(jnp.float32) - obs_mean, 0.0).astype(jnp.bfloat16)
    departure = jnp.where(valid, obs_value - obs_mean, 0.0)
    aux_window = extended(jnp.stack([departure, obs_prec, obs_pos]), (("grid", 1),), obs_blocks)
    grid_pos = lax.axis_index("grid")
    total_obs = obs_blocks * grid_count
    nb_total = blocks_dev * grid_count
    slot_count = obs_prior.shape[2] // mem_count
    mine = lax.all_to_all(perturb, "mem", split_axis=2, concat_axis=0, tiled=True)
    window = extended(mine, (("grid", 1),), obs_blocks)
    aux_part = lax.dynamic_slice_in_dim(
        aux_window, lax.axis_index("mem") * slot_count, slot_count, 2
    )
    all_ids = (pair_block - (grid_pos - 1) * obs_blocks) % total_obs
    all_centers = (grid_pos * blocks_dev + jnp.arange(blocks_dev, dtype=jnp.int32)).astype(
        jnp.float32
    ) + 0.5

    def share_one(block_ids, center):
        return block_terms(window, aux_part, block_ids, center, nb_total)

    grams, forcings = run_groups(share_one, (all_ids, all_centers), blocks_dev)
    gram_own, forcing_own = (
        lax.psum_scatter(grams, "mem", scatter_dimension=0, tiled=True),
        lax.psum_scatter(forcings, "mem", scatter_dimension=0, tiled=True),
    )
    transforms = run_groups(finish, (gram_own, forcing_own), owned)
    deviation = (ens_state.astype(jnp.float32) - state_mean).astype(jnp.bfloat16)
    rows_back = lax.all_to_all(transforms, "mem", split_axis=1, concat_axis=0, tiled=True)
    product = lax.dot_general(
        rows_back, deviation, (((1,), (0,)), ((0,), (1,))), preferred_element_type=jnp.float32
    )
    summed = lax.psum_scatter(
        jnp.transpose(product, (1, 0, 2)), "mem", scatter_dimension=0, tiled=True
    )
    return (state_mean[None, :, :] + summed).astype(jnp.bfloat16)


def solution(mesh):
    placed = (
        P("mem", "grid", None),
        P("mem", "grid", None),
        P("grid", None),
        P("grid", None),
        P("grid"),
        P("grid", None),
        P("grid", None),
    )
    return jax.shard_map(
        per_device, mesh=mesh, in_specs=placed, out_specs=P("mem", "grid", None), check_vma=False
    )
```

profile of v0, /device:TPU:0, one launch (start us, length us, event | category | flops | bytes accessed | tf_op | source)
XLA Modules:
  0.0 495.5 jit_solution(2000154030218237241)
XLA Ops:
  6.5 3.2 copy.82
  9.8 1.6 convert_reduce_fusion
  11.6 45.0 %all-reduce.4.cloned.1.call-done = f32[384,128]{0,1:T(8,128)} async-done(((f32[384,128]{0,1:T(8,128)}), f32[384,128]{0,1:T(8,128)}) %all-reduce.4.cloned.1.call-update) | async-done | bytes 196624 | tf_op jit(solution)/shard_map/psum | solution.py:81
  57.6 1.1 fusion.37
  58.8 30.5 %all_to_all.36 = bf16[20,384,128]{1,0,2:T(8,128)(2,1)S(1)} all-to-all(bf16[20,384,128]{1,0,2:T(8,128)(2,1)S(1)} %fusion.37), channel_id=1, replica_groups=mesh['mem'=4,'grid'=8] {'mem'}, dimensions={2} | all-to-all | bytes 3932160 | tf_op jit(solution)/shard_map/all_to_all | solution.py:98
  92.5 2.9 collective-permute-start.3
  96.6 52.7 %collective-permute-done.2 = f32[3,384,128]{1,2,0:T(8,128)S(1)} collective-permute-done((f32[3,384,128]{1,2,0:T(8,128)}, f32[3,384,128]{1,2,0:T(8,128)S(1)}, u32[]{:S(2)}, u32[]{:S(2)}) %collective-permute-start.2) | collective-permute-done | bytes 589856 | tf_op jit(solution)/shard_map/ppermute | solution.py:21
  151.2 1.8 copy.90
  152.9 5.2 %pad_maximum_fusion = bf16[80,1152,32]{1,2,0:T(8,128)(2,1)} fusion(bf16[80,384,32]{1,2,0:T(8,128)(2,1)} %collective-permute-done.1, bf16[80,384,32]{1,2,0:T(8,128)(2,1)S(1)} %bitcast.224, bf16[80,384,32]{1,2,0:T(8,128)(2,1)} %collective-permute-done), kind=kLoop, calls=%fused_computation.58 | loop fusion | flops 17694720 | bytes 11796480 | tf_op jit(solution)/shard_map/concatenate | solution.py:25
  158.1 13.1 %copy.89 = bf16[80,1152,32]{0,2,1:T(8,128)(2,1)} copy(bf16[80,1152,32]{1,2,0:T(8,128)(2,1)} %pad_maximum_fusion) | data formatting | bytes 11796480 | tf_op jit(solution)/shard_map/while | solution.py:70
  171.2 230.2 %while.24 = (s32[]{:T(128)}, f32[8,2,80,80]{3,2,1,0:T(8,128)}, f32[8,2,80]{2,1,0:T(2,128)S(1)}, s32[8,2,256]{2,1,0:T(2,128)}, bf16[80,1152,32]{0,2,1:T(8,128)(2,...) while((s32[]{:T(128)}, f32[8,2,80,80]{3,2,1,0:T(8,128)}, f32[8,2,80]{2,1,0:T(2,128)S(1)}, ...), condition=%wide.region_5.7_spmd, body=%wide.region_4.6_spmd.sunk | while | flops 237428736 | bytes 31159080 | solution.py:70
  171.9 7.0 %gather_fusion = bf16[512,80,32]{1,2,0:T(8,128)(2,1)} fusion(bf16[80,1152,32]{0,2,1:T(8,128)(2,1)} %get-tuple-element.285, s32[1024]{0:T(1024)S(1)} %pad_clamp_fusion.4), kind=kCustom, calls=%fused_computation.3.clone.1 | custom fusion | bytes 5244928 | tf_op jit(solution)/shard_map/while/body/eval_jaxpr/vmap(jit(_take))/gather | solution.py:49
  178.9 7.1 %copy.119 = bf16[2,256,80,32]{1,2,3,0:T(8,128)(2,1)} copy(bf16[2,256,80,32]{2,3,1,0:T(8,128)(2,1)} %bitcast.217) | data formatting | bytes 5242880 | tf_op jit(solution)/shard_map/while/body/eval_jaxpr/vmap(jit(_take))/gather | solution.py:49
  186.7 1.5 slice_bitcast_fusion.4
  192.0 4.1 fusion.107
  197.8 2.1 fusion.108
  200.7 7.0 %gather_fusion = bf16[512,80,32]{1,2,0:T(8,128)(2,1)} fusion(bf16[80,1152,32]{0,2,1:T(8,128)(2,1)} %get-tuple-element.285, s32[1024]{0:T(1024)S(1)} %pad_clamp_fusion.4), kind=kCustom, calls=%fused_computation.3.clone.1 | custom fusion | bytes 5244928 | tf_op jit(solution)/shard_map/while/body/eval_jaxpr/vmap(jit(_take))/gather | solution.py:49
  207.7 7.1 %copy.119 = bf16[2,256,80,32]{1,2,3,0:T(8,128)(2,1)} copy(bf16[2,256,80,32]{2,3,1,0:T(8,128)(2,1)} %bitcast.217) | data formatting | bytes 5242880 | tf_op jit(solution)/shard_map/while/body/eval_jaxpr/vmap(jit(_take))/gather | solution.py:49
  215.5 1.5 slice_bitcast_fusion.4
  220.8 4.1 fusion.107
  226.6 2.1 fusion.108
  229.5 7.0 %gather_fusion = bf16[512,80,32]{1,2,0:T(8,128)(2,1)} fusion(bf16[80,1152,32]{0,2,1:T(8,128)(2,1)} %get-tuple-element.285, s32[1024]{0:T(1024)S(1)} %pad_clamp_fusion.4), kind=kCustom, calls=%fused_computation.3.clone.1 | custom fusion | bytes 5244928 | tf_op jit(solution)/shard_map/while/body/eval_jaxpr/vmap(jit(_take))/gather | solution.py:49
  236.4 7.1 %copy.119 = bf16[2,256,80,32]{1,2,3,0:T(8,128)(2,1)} copy(bf16[2,256,80,32]{2,3,1,0:T(8,128)(2,1)} %bitcast.217) | data formatting | bytes 5242880 | tf_op jit(solution)/shard_map/while/body/eval_jaxpr/vmap(jit(_take))/gather | solution.py:49
  244.3 1.5 slice_bitcast_fusion.4
  249.6 4.1 fusion.107
  255.4 2.1 fusion.108
  258.3 7.0 %gather_fusion = bf16[512,80,32]{1,2,0:T(8,128)(2,1)} fusion(bf16[80,1152,32]{0,2,1:T(8,128)(2,1)} %get-tuple-element.285, s32[1024]{0:T(1024)S(1)} %pad_clamp_fusion.4), kind=kCustom, calls=%fused_computation.3.clone.1 | custom fusion | bytes 5244928 | tf_op jit(solution)/shard_map/while/body/eval_jaxpr/vmap(jit(_take))/gather | solution.py:49
  265.2 7.1 %copy.119 = bf16[2,256,80,32]{1,2,3,0:T(8,128)(2,1)} copy(bf16[2,256,80,32]{2,3,1,0:T(8,128)(2,1)} %bitcast.217) | data formatting | bytes 5242880 | tf_op jit(solution)/shard_map/while/body/eval_jaxpr/vmap(jit(_take))/gather | solution.py:49
  273.1 1.5 slice_bitcast_fusion.4
  278.4 4.1 fusion.107
  284.2 2.1 fusion.108
  287.0 7.0 %gather_fusion = bf16[512,80,32]{1,2,0:T(8,128)(2,1)} fusion(bf16[80,1152,32]{0,2,1:T(8,128)(2,1)} %get-tuple-element.285, s32[1024]{0:T(1024)S(1)} %pad_clamp_fusion.4), kind=kCustom, calls=%fused_computation.3.clone.1 | custom fusion | bytes 5244928 | tf_op jit(solution)/shard_map/while/body/eval_jaxpr/vmap(jit(_take))/gather | solution.py:49
  294.0 7.1 %copy.119 = bf16[2,256,80,32]{1,2,3,0:T(8,128)(2,1)} copy(bf16[2,256,80,32]{2,3,1,0:T(8,128)(2,1)} %bitcast.217) | data formatting | bytes 5242880 | tf_op jit(solution)/shard_map/while/body/eval_jaxpr/vmap(jit(_take))/gather | solution.py:49
  301.8 1.5 slice_bitcast_fusion.4
  307.1 4.1 fusion.107
  313.0 2.1 fusion.108
  315.8 7.0 %gather_fusion = bf16[512,80,32]{1,2,0:T(8,128)(2,1)} fusion(bf16[80,1152,32]{0,2,1:T(8,128)(2,1)} %get-tuple-element.285, s32[1024]{0:T(1024)S(1)} %pad_clamp_fusion.4), kind=kCustom, calls=%fused_computation.3.clone.1 | custom fusion | bytes 5244928 | tf_op jit(solution)/shard_map/while/body/eval_jaxpr/vmap(jit(_take))/gather | solution.py:49
  322.8 7.1 %copy.119 = bf16[2,256,80,32]{1,2,3,0:T(8,128)(2,1)} copy(bf16[2,256,80,32]{2,3,1,0:T(8,128)(2,1)} %bitcast.217) | data formatting | bytes 5242880 | tf_op jit(solution)/shard_map/while/body/eval_jaxpr/vmap(jit(_take))/gather | solution.py:49
  330.6 1.5 slice_bitcast_fusion.4
  335.9 4.1 fusion.107
  341.7 2.1 fusion.108
  344.6 7.0 %gather_fusion = bf16[512,80,32]{1,2,0:T(8,128)(2,1)} fusion(bf16[80,1152,32]{0,2,1:T(8,128)(2,1)} %get-tuple-element.285, s32[1024]{0:T(1024)S(1)} %pad_clamp_fusion.4), kind=kCustom, calls=%fused_computation.3.clone.1 | custom fusion | bytes 5244928 | tf_op jit(solution)/shard_map/while/body/eval_jaxpr/vmap(jit(_take))/gather | solution.py:49
  351.5 7.1 %copy.119 = bf16[2,256,80,32]{1,2,3,0:T(8,128)(2,1)} copy(bf16[2,256,80,32]{2,3,1,0:T(8,128)(2,1)} %bitcast.217) | data formatting | bytes 5242880 | tf_op jit(solution)/shard_map/while/body/eval_jaxpr/vmap(jit(_take))/gather | solution.py:49
  359.4 1.5 slice_bitcast_fusion.4
  364.7 4.1 fusion.107
  370.5 2.1 fusion.108
  373.4 7.0 %gather_fusion = bf16[512,80,32]{1,2,0:T(8,128)(2,1)} fusion(bf16[80,1152,32]{0,2,1:T(8,128)(2,1)} %get-tuple-element.285, s32[1024]{0:T(1024)S(1)} %pad_clamp_fusion.4), kind=kCustom, calls=%fused_computation.3.clone.1 | custom fusion | bytes 5244928 | tf_op jit(solution)/shard_map/while/body/eval_jaxpr/vmap(jit(_take))/gather | solution.py:49
  380.3 7.1 %copy.119 = bf16[2,256,80,32]{1,2,3,0:T(8,128)(2,1)} copy(bf16[2,256,80,32]{2,3,1,0:T(8,128)(2,1)} %bitcast.217) | data formatting | bytes 5242880 | tf_op jit(solution)/shard_map/while/body/eval_jaxpr/vmap(jit(_take))/gather | solution.py:49
  388.1 1.5 slice_bitcast_fusion.4
  393.5 4.1 fusion.107
  399.3 2.1 fusion.108
  401.5 1.2 dynamic-slice
  404.4 15.5 %all-reduce.1 = (f32[16,80]{1,0:T(8,128)S(1)}, f32[16,512]{1,0:T(8,128)S(1)}) all-reduce(f32[16,80]{1,0:T(8,128)S(1)} %bitcast.239, f32[16,512]{1,0:T(8,128)S(1)} %convert_reduce_fusion.1), channel_id=3, replica_groups=mesh['mem'=4,'grid'=8] {'mem'}, use_global_device_ids=true, to_apply=%region_7.9.clone | all-reduce | flops 9472 | bytes 75776
  419.9 4.9 reduce-scatter.3.cloned.1.call-done
  424.8 10.8 %while.25 = (s32[]{:T(128)}, bf16[2,2,80,80]{3,2,1,0:T(8,128)(2,1)S(1)}, f32[2,2,80,80]{3,2,1,0:T(8,128)}, f32[2,2,80]{2,1,0:T(2,128)S(1)}, s32[]{:T(128)}, /*index=5*/f32[]{:T(128)}) while((s32[]{:T(128)}, bf16[2,2,80,80]{3,2,1,0:T(8,128)(2,1)S(1)}, f32[2,2,80,80]{3,2,1,0:T(8,128)}, f32[2,2,80]{2,1,0:T(2,128)S(1)}, s32[]{:T(128)}, ...), condition=%wide.region_11.13_spmd, body=%wide.region_8.12_spmd.sunk | while | flops 98860800 | bytes 1675413 | solution.py:70
  426.0 1.1 fusion.130
  427.3 1.2 fusion.132
  431.4 1.1 fusion.130
  432.7 1.2 fusion.132
  436.3 3.3 all-to-all-start.1
  439.7 4.7 all-to-all-done.1
  445.0 3.0 copy.94
  448.1 39.0 %reduce-scatter.5.cloned.1.call-done = f32[20,16,512]{2,1,0:T(8,128)} async-done(((f32[80,16,512]{2,1,0:T(8,128)}), f32[20,16,512]{2,1,0:T(8,128)}) %reduce-scatter.5.cloned.1.call-update) | async-done | bytes 655376 | tf_op jit(solution)/shard_map/reduce_scatter | solution.py:122
  487.1 1.9 add_convert_fusion.1
  (227 shorter events, 71.0 us)
Async XLA Ops:
  6.5 4.9 copy-start.3
  6.5 50.1 %all-reduce.4.cloned.1.call-start = ((), (), s32[]{:S(2)}) async-start(), calls=%async_computation.4 | async-start | bytes 393216 | tf_op jit(solution)/shard_map/psum | solution.py:81
  9.8 1.8 copy-start.7
  11.4 413.4 %reduce-scatter.3.cloned.1.call-start = ((), (), s32[]{:S(2)}) async-start(), calls=%async_computation.5 | async-start | bytes 819200 | tf_op jit(solution)/shard_map/reduce_scatter | solution.py:113
  89.3 1.4 copy-start.4
  89.3 1.5 copy-start.5
  89.3 6.1 %copy-start.6 = (s32[16,256]{1,0:T(8,128)S(1)}, s32[16,256]{1,0:T(8,128)}, u32[]{:S(2)}) copy-start(s32[16,256]{1,0:T(8,128)} %param.18) | copy-start | bytes 49156
  89.6 63.3 %collective-permute-start.1 = (bf16[80,384,32]{1,2,0:T(8,128)(2,1)S(1)}, bf16[80,384,32]{1,2,0:T(8,128)(2,1)}, u32[]{:S(2)}, u32[]{:S(2)}) collective-permute-start(bf16[80,384,32]{1,2,0:T(8,128)(2,1)S(1)} %bitcast.222), channel_id=1, source_target_pairs={{1,0},{2,1},{3,2},{4,3},{5,4},{6,5},{7,6},{0,7},{9,8},{10,9},{11,1... | collective-permute-start | bytes 5898248 | tf_op jit(solution)/shard_map/ppermute | solution.py:24
  90.7 62.2 %collective-permute-start = (bf16[80,384,32]{1,2,0:T(8,128)(2,1)S(1)}, bf16[80,384,32]{1,2,0:T(8,128)(2,1)}, u32[]{:S(2)}, u32[]{:S(2)}) collective-permute-start(bf16[80,384,32]{1,2,0:T(8,128)(2,1)S(1)} %bitcast.223), channel_id=1, source_target_pairs={{0,1},{1,2},{2,3},{3,4},{4,5},{5,6},{6,7},{7,0},{8,9},{9,10},{10,1... | collective-permute-start | bytes 5898248 | tf_op jit(solution)/shard_map/ppermute | solution.py:21
  91.8 57.5 %collective-permute-start.2 = (f32[3,384,128]{1,2,0:T(8,128)}, f32[3,384,128]{1,2,0:T(8,128)S(1)}, u32[]{:S(2)}, u32[]{:S(2)}) collective-permute-start(f32[3,384,128]{1,2,0:T(8,128)} %pad_maximum_fusion.1), channel_id=1, source_target_pairs={{0,1},{1,2},{2,3},{3,4},{4,5},{5,6},{6,7},{7,0},{8,9},{9,10},{10,1... | collective-permute-start | bytes 1769480 | tf_op jit(solution)/shard_map/ppermute | solution.py:21
  92.5 57.7 %collective-permute-start.3 = (f32[3,384,128]{1,2,0:T(8,128)}, f32[3,384,128]{1,2,0:T(8,128)}, u32[]{:S(2)}, u32[]{:S(2)}) collective-permute-start(f32[3,384,128]{1,2,0:T(8,128)} %pad_maximum_fusion.1), channel_id=1, source_target_pairs={{1,0},{2,1},{3,2},{4,3},{5,4},{6,5},{7,6},{0,7},{9,8},{10,9},{11,1... | collective-permute-start | bytes 1769480 | tf_op jit(solution)/shard_map/ppermute | solution.py:24
  149.3 0.8 copy-start.2
  196.1 1.7 copy-start
  224.9 1.7 copy-start
  253.7 1.7 copy-start
  282.4 1.7 copy-start
  311.2 1.7 copy-start
  340.0 1.7 copy-start
  368.8 1.7 copy-start
  397.5 1.7 copy-start
  424.8 14.9 %copy-start.1 = (bf16[20,16,512]{2,1,0:T(8,128)(2,1)S(1)}, bf16[20,16,512]{2,1,0:T(8,128)(2,1)}, u32[]{:S(2)}) copy-start(bf16[20,16,512]{2,1,0:T(8,128)(2,1)} %param.13) | copy-start | bytes 983044
  436.3 8.2 %all-to-all-start.1 = ((bf16[4,80,80]{2,0,1:T(4,128)(2,1)}), bf16[4,80,80]{2,0,1:T(4,128)(2,1)S(1)}, u32[]{:S(2)}, u32[]{:S(2)}) async-start(bf16[4,80,80]{2,0,1:T(4,128)(2,1)} %copy.91), calls=%async_computation.2 | async-start | bytes 163840 | tf_op jit(solution)/shard_map/all_to_all | solution.py:118
  439.6 47.5 %reduce-scatter.5.cloned.1.call-start = ((), (), s32[]{:S(2)}) async-start(), calls=%async_computation.6 | async-start | bytes 3276800 | tf_op jit(solution)/shard_map/reduce_scatter | solution.py:122
Sparse Core Ops, SparseCore 0:
  11.5 45.1 all-reduce.3
  401.6 23.1 reduce-scatter.2
  448.2 38.8 reduce-scatter.4
where the time goes:
time: 499 us; the launch traced here: 496 us
  local copies, waits for them, and re-layouts  187 us (37%)
  waiting for transfers between devices  146 us (29%)
  matrix products  58.2 us (12%)
  blocking collectives  46 us (9%)
  other arithmetic  35.6 us (7%)
  between operations  13.9 us (3%)
  starting transfers between devices  8.01 us (2%)
    gather x16, local copies, waits for them, and re-layouts, block_terms(): chosen = jnp.take(window, block_ids, axis=1)  113 us
    ppermute x2, waiting for transfers between devices, extended(): lax.ppermute(lax.slice_in_dim(block, block.shape[dim] - width, None, axis...  52.7 us
    psum x1, waiting for transfers between devices, per_device(): lax.psum((jnp.sum(obs_prior, axis=0, dtype=jnp.float32), jnp.sum(ens_stat...  45 us
    reduce_scatter x1, waiting for transfers between devices, per_device(): lax.psum_scatter(jnp.transpose(product, (1, 0, 2)), 'mem', scatter_dimens...  39 us
    dot_general x8, matrix products, block_terms(): lax.dot_general(scaled, chosen, (((1, 2), (1, 2)), ((), ())), preferred_e...  32.6 us
    all_to_all x1, blocking collectives, per_device(): lax.all_to_all(perturb, 'mem', split_axis=2, concat_axis=0, tiled=True)  30.5 us
    dot_general x8, matrix products, block_terms(): jnp.einsum('ipk,pk->i', scaled.astype(jnp.float32), departure, precision=...  17 us
    unnamed x1, blocking collectives  15.5 us
  transfers between devices with their start and end apart: 8, of which 5 were waited for; matrix products, arithmetic and copies ran while one was open for 2% of the time, Pallas kernels for 0%

commit v1 on v0

v1 whole, which is shorter than its diff:
```python
import functools
import math

import jax
import jax.numpy as jnp
from jax import lax
from jax.experimental import pallas as pl
from jax.experimental.pallas import tpu as pltpu
from jax.sharding import PartitionSpec as P

NSIT = 3
LOCR = 8
inflation = 1.1

LANES = 128
ROWS = 16
GROUP = 8
MESH = pl.DeviceIdType.MESH
HIGHEST = lax.Precision.HIGHEST


def kernel(
    dims,
    ens_ref, obs_ref, aux_ref, pair_ref,
    out_ref,
    prior, dev, weight, aux, pairs, scaled, gram, near_send, near_recv,
    share_send, share_recv, ens_all, result,
    local_sem, obs_send, obs_recv, ens_send, ens_recv, pair_send, pair_recv,
    near_ssem, near_rsem, share_ssem, share_rsem, out_ssem, out_rsem,
):
    peers, ring, part, chunks, owned, blocks, members, pad, extra = dims
    mem = lax.axis_index("mem")
    grid = lax.axis_index("grid")
    left = lax.rem(grid + ring - 1, ring)
    right = lax.rem(grid + 1, ring)
    share = chunks * ROWS
    nb_total = blocks * ring
    obs_dev_blocks = share * peers
    slots = obs_ref.shape[2]

    def peer(step):
        return lax.rem(mem + step, peers)

    def at_peer(step):
        return (peer(step), grid)

    def obs_copy(chunk, step):
        return pltpu.make_async_remote_copy(
            src_ref=obs_ref.at[:, pl.ds(peer(step) * share + chunk * ROWS, ROWS), :],
            dst_ref=prior.at[chunk, pl.ds(mem * part, part)],
            send_sem=obs_send.at[chunk, step - 1],
            recv_sem=obs_recv.at[chunk, step - 1],
            device_id=at_peer(step),
            device_id_type=MESH,
        )

    def obs_own(chunk):
        return pltpu.make_async_copy(
            obs_ref.at[:, pl.ds(mem * share + chunk * ROWS, ROWS), :],
            prior.at[chunk, pl.ds(mem * part, part)],
            local_sem.at[2 + chunk],
        )

    def ens_copy(step):
        return pltpu.make_async_remote_copy(
            src_ref=ens_ref.at[pl.ds(peer(step) * owned, owned)],
            dst_ref=ens_all.at[mem],
            send_sem=ens_send.at[step - 1],
            recv_sem=ens_recv.at[step - 1],
            device_id=at_peer(step),
            device_id_type=MESH,
        )

    def pair_copy(side):
        return pltpu.make_async_remote_copy(
            src_ref=pair_ref,
            dst_ref=pairs.at[2 - 2 * side],
            send_sem=pair_send.at[side],
            recv_sem=pair_recv.at[side],
            device_id=(mem, left if side == 0 else right),
            device_id_type=MESH,
        )

    def near_copy(side):
        return pltpu.make_async_remote_copy(
            src_ref=near_send.at[side],
            dst_ref=near_recv.at[side],
            send_sem=near_ssem.at[side],
            recv_sem=near_rsem.at[side],
            device_id=(mem, left if side == 0 else right),
            device_id_type=MESH,
        )

    def share_copy(step):
        return pltpu.make_async_remote_copy(
            src_ref=share_send.at[peer(step)],
            dst_ref=share_recv.at[step - 1],
            send_sem=share_ssem.at[step - 1],
            recv_sem=share_rsem.at[step - 1],
            device_id=at_peer(step),
            device_id_type=MESH,
        )

    def out_copy(step):
        return pltpu.make_async_remote_copy(
            src_ref=result.at[peer(step)],
            dst_ref=out_ref.at[pl.ds(mem * owned, owned)],
            send_sem=out_ssem.at[step - 1],
            recv_sem=out_rsem.at[step - 1],
            device_id=at_peer(step),
            device_id_type=MESH,
        )

    aux_own = pltpu.make_async_copy(
        aux_ref.at[:, pl.ds(mem * share, share), :], aux, local_sem.at[0]
    )
    ens_own = pltpu.make_async_copy(
        ens_ref.at[pl.ds(mem * owned, owned)], ens_all.at[mem], local_sem.at[1]
    )
    pair_own = pltpu.make_async_copy(pair_ref, pairs.at[1], local_sem.at[2 + chunks])
    aux_own.start()
    ens_own.start()
    pair_own.start()
    for chunk in range(chunks):
        obs_own(chunk).start()

    barrier = pltpu.get_barrier_semaphore()
    for step in range(1, peers):
        pl.semaphore_signal(barrier, inc=1, device_id=at_peer(step), device_id_type=MESH)
    for side in (left, right):
        pl.semaphore_signal(barrier, inc=1, device_id=(mem, side), device_id_type=MESH)
    pl.semaphore_wait(barrier, peers + 1)

    for side in range(2):
        pair_copy(side).start()
    for chunk in range(chunks):
        for step in range(1, peers):
            obs_copy(chunk, step).start()
    for step in range(1, peers):
        ens_copy(step).start()

    aux_own.wait()
    pair_own.wait()
    for side in range(2):
        pair_copy(side).wait()

    first_block = grid * obs_dev_blocks + mem * share

    def weigh(block, _):
        third = block // blocks
        home = lax.rem(grid + third + ring - 1, ring)
        inner = block - third * blocks
        center = (home * blocks + inner).astype(jnp.float32) + 0.5
        ids = lax.broadcasted_iota(jnp.int32, (share, pairs.shape[2]), 0) + first_block
        listed = pairs[third, pl.ds(inner, 1), :] == ids
        chosen = jnp.max(listed.astype(jnp.float32), axis=1, keepdims=True)
        distance = jnp.abs(aux[2] - center)
        distance = jnp.minimum(distance, nb_total - distance)
        relative = distance / LOCR
        value = aux[1] * jnp.exp(-0.5 * relative * relative)
        weight[block] = (value * chosen).reshape(chunks, ROWS, slots)
        return 0

    lax.fori_loop(0, 3 * blocks, weigh, 0)

    def perturb(chunk):
        obs_own(chunk).wait()
        for step in range(1, peers):
            obs_copy(chunk, step).wait()
        values = prior[chunk].astype(jnp.float32)
        mean = jnp.sum(values, axis=0) / members
        rows = pl.ds(pl.multiple_of(chunk * ROWS, ROWS), ROWS)
        slot = lax.broadcasted_iota(jnp.int32, (ROWS, slots), 1).astype(jnp.float32)
        valid = slot < aux[3, rows, :]
        moved = jnp.where(valid[None], values - mean[None], 0.0)
        departure = jnp.where(valid, aux[0, rows, :] - mean, 0.0)
        high = departure.astype(jnp.bfloat16).astype(jnp.float32)
        rest = jnp.zeros((extra - 2, ROWS, slots), jnp.float32)
        whole = jnp.concatenate([moved, high[None], (departure - high)[None], rest], axis=0)
        turned = jnp.transpose(whole, (1, 0, 2)).astype(jnp.bfloat16)
        for row in range(ROWS):
            dev[chunk, :, row * slots : (row + 1) * slots] = turned[row]

    def products(group, chunk, first):
        start = group * GROUP
        for row in range(ROWS):
            here = slice(row * slots, (row + 1) * slots)
            tile = dev[chunk, 0:members, here]
            for block in range(GROUP):
                line = weight[start + block, chunk, row : row + 1, :]
                line = jnp.broadcast_to(line, (16, slots)).astype(jnp.bfloat16)
                line = jnp.concatenate([line] * (members // 16), axis=0)
                scaled[block * members : (block + 1) * members, here] = tile * line
        product = lax.dot_general(
            scaled[...], dev[chunk], (((1,), (1,)), ((), ())), preferred_element_type=jnp.float32
        )
        product = product.reshape(GROUP, members, members + extra)
        where = pl.ds(start, GROUP)
        if first:
            gram[where, :, 0 : members + extra] = product
        else:
            gram[where, :, 0 : members + extra] += product

    groups = blocks // GROUP

    def over(groups_here, chunk, first):
        def one(index, _):
            products(groups_here(index), chunk, first)
            return 0
        return one

    def outer(index):
        return index + (index // groups) * groups

    gram[...] = jnp.zeros_like(gram)

    def arrive(chunk, _):
        perturb(chunk)
        lax.fori_loop(0, 2 * groups, over(outer, chunk, False), 0)
        return 0

    lax.fori_loop(0, chunks, arrive, 0)
    for side in range(2):
        near_send[side] = gram[pl.ds(2 * side * blocks, blocks)].astype(jnp.bfloat16)
        near_copy(side).start()

    def inside(chunk, _):
        lax.fori_loop(0, groups, over(lambda index: groups + index, chunk, False), 0)
        return 0

    lax.fori_loop(0, chunks, inside, 0)
    for side in range(2):
        near_copy(side).wait()

    total = (
        gram[pl.ds(blocks, blocks)]
        + near_recv[0].astype(jnp.float32)
        + near_recv[1].astype(jnp.float32)
    )
    gram[pl.ds(blocks, blocks)] = total
    share_send[...] = total.reshape(peers, owned, members, LANES).astype(jnp.bfloat16)
    for step in range(1, peers):
        share_copy(step).start()
    ens_own.wait()
    for step in range(1, peers):
        ens_copy(step).wait()
    for step in range(1, peers):
        share_copy(step).wait()

    width = LANES
    line = lax.broadcasted_iota(jnp.int32, (width, width), 0)
    lane = lax.broadcasted_iota(jnp.int32, (width, width), 1)
    eye = jnp.where((line == lane) & (line < members), 1.0, 0.0).astype(jnp.float32)
    square = (line < members) & (lane < members)
    padded = (line // pad) * part + lax.rem(line, pad)
    spread = jnp.where((padded == lane) & (lax.rem(line, pad) < part), 1.0, 0.0).astype(jnp.bfloat16)
    dot = functools.partial(jnp.dot, precision=HIGHEST, preferred_element_type=jnp.float32)

    y_iter, z_iter, bound, push = [], [], [], []
    for own in range(owned):
        part_sum = gram[blocks + mem * owned + own]
        for step in range(1, peers):
            part_sum = part_sum + share_recv[step - 1, own].astype(jnp.float32)
        part_sum = jnp.concatenate(
            [part_sum, jnp.zeros((width - members, LANES), jnp.float32)], axis=0
        )
        forcing = jnp.where((lane == members) | (lane == members + 1), part_sum, 0.0)
        forcing = jnp.sum(forcing, axis=1, keepdims=True)
        system = jnp.where(square, part_sum, 0.0) + (members - 1) / inflation * eye
        sums = jnp.sum(jnp.abs(system), axis=1, keepdims=True)
        most = jnp.max(sums, axis=0, keepdims=True)
        bound.append(most)
        push.append(jnp.broadcast_to(forcing, (width, width)))
        y_iter.append(system / most)
        z_iter.append(eye)
    every = range(owned)
    for sweep in range(NSIT):
        if sweep == 0:
            factor = [1.5 * eye - 0.5 * y_iter[o] for o in every]
            z_iter = factor
        else:
            factor = [1.5 * eye - 0.5 * dot(z_iter[o], y_iter[o]) for o in every]
            z_iter = [dot(factor[o], z_iter[o]) for o in every]
        if sweep < NSIT - 1:
            y_iter = [dot(y_iter[o], factor[o]) for o in every]
    root = [z_iter[o] / jnp.sqrt(bound[o]) for o in every]
    once = [dot(root[o], push[o]) for o in every]
    twice = [dot(root[o], once[o]) for o in every]
    for own in range(owned):
        transform = jnp.where(square, math.sqrt(members - 1) * root[own] + twice[own], 0.0)
        turned = jnp.transpose(transform).astype(jnp.bfloat16)
        turned = jnp.dot(spread, turned, preferred_element_type=jnp.float32).astype(jnp.bfloat16)
        turned = lax.dot_general(
            turned, spread, (((1,), (1,)), ((), ())), preferred_element_type=jnp.float32
        ).astype(jnp.bfloat16)
        state = ens_all[:, own].astype(jnp.float32).reshape(peers * pad, -1)
        mean = jnp.sum(state, axis=0, keepdims=True) / members
        deviation = (state - mean).astype(jnp.bfloat16)
        moved = jnp.dot(turned, deviation, preferred_element_type=jnp.float32)
        analysis = (mean + moved).astype(jnp.bfloat16)
        result[:, own] = analysis.reshape(peers, pad, -1)

    for step in range(1, peers):
        out_copy(step).start()
    out_own = pltpu.make_async_copy(
        result.at[mem], out_ref.at[pl.ds(mem * owned, owned)], local_sem.at[0]
    )
    out_own.start()
    out_own.wait()
    for step in range(1, peers):
        out_copy(step).wait()


def per_device(ens_state, obs_prior, obs_value, obs_prec, obs_len, pair_block, obs_pos):
    peers = lax.axis_size("mem")
    ring = lax.axis_size("grid")
    part, blocks, length = ens_state.shape
    members = peers * part
    slots = obs_prior.shape[2]
    share = obs_prior.shape[1] // peers
    chunks = share // ROWS
    owned = blocks // peers
    pad = LANES // peers
    extra = 16
    dims = (peers, ring, part, chunks, owned, blocks, members, pad, extra)

    ens = jnp.pad(jnp.transpose(ens_state, (1, 0, 2)), ((0, 0), (0, pad - part), (0, 0)))
    counts = jnp.broadcast_to(obs_len.astype(jnp.float32)[:, None], obs_value.shape)
    aux = jnp.stack([obs_value, obs_prec, obs_pos, counts])

    bf16, f32 = jnp.bfloat16, jnp.float32
    others = peers - 1
    dma = pltpu.SemaphoreType.DMA
    anywhere = pl.BlockSpec(memory_space=pl.ANY)
    out = pl.pallas_call(
        functools.partial(kernel, dims),
        out_shape=jax.ShapeDtypeStruct((blocks, pad, length), bf16),
        in_specs=[anywhere] * 4,
        out_specs=anywhere,
        scratch_shapes=[
            pltpu.VMEM((chunks, members, ROWS, slots), bf16),
            pltpu.VMEM((chunks, members + extra, ROWS * slots), bf16),
            pltpu.VMEM((3 * blocks, chunks, ROWS, slots), f32),
            pltpu.VMEM((4, share, slots), f32),
            pltpu.VMEM((3,) + pair_block.shape, jnp.int32),
            pltpu.VMEM((GROUP * members, ROWS * slots), bf16),
            pltpu.VMEM((3 * blocks, members, LANES), f32),
            pltpu.VMEM((2, blocks, members, LANES), bf16),
            pltpu.VMEM((2, blocks, members, LANES), bf16),
            pltpu.VMEM((peers, owned, members, LANES), bf16),
            pltpu.VMEM((others, owned, members, LANES), bf16),
            pltpu.VMEM((peers, owned, pad, length), bf16),
            pltpu.VMEM((peers, owned, pad, length), bf16),
            dma((3 + chunks,)),
            dma((chunks, others)),
            dma((chunks, others)),
            dma((others,)),
            dma((others,)),
            dma((2,)),
            dma((2,)),
            dma((2,)),
            dma((2,)),
            dma((others,)),
            dma((others,)),
            dma((others,)),
            dma((others,)),
        ],
        compiler_params=pltpu.CompilerParams(
            collective_id=0, has_side_effects=True, vmem_limit_bytes=48 * 2**20
        ),
    )(ens, obs_prior, aux, pair_block)
    return jnp.transpose(out[:, :part, :], (1, 0, 2))


def solution(mesh):
    placed = (
        P("mem", "grid", None),
        P("mem", "grid", None),
        P("grid", None),
        P("grid", None),
        P("grid"),
        P("grid", None),
        P("grid", None),
    )
    return jax.shard_map(
        per_device, mesh=mesh, in_specs=placed, out_specs=P("mem", "grid", None), check_vma=False
    )
```

time: 499 us -> 65.1 us (0.13)
  local copies, waits for them, and re-layouts: 187 us -> 2.19 us
  waiting for transfers between devices: 146 us -> 0 us
  Pallas kernels: 0 us -> 61.8 us
  matrix products: 58.2 us -> 0 us
  blocking collectives: 46 us -> 0 us
  other arithmetic: 35.6 us -> 0.89 us
  between operations: 13.9 us -> 0.09 us
  starting transfers between devices: 8.01 us -> 0 us
    gather x56 -> x0, local copies, waits for them, and re-layouts: 139 us -> none  [the longest x16 113 us: block_terms(): chosen = jnp.take(window, block_ids, axis=1)]
    pallas_call x0 -> x1, Pallas kernels: none -> 61.8 us  [per_device(): pl.pallas_call(functools.partial(kernel, dims), out_shape=jax.ShapeDtypeS...]
    dot_general x37 -> x0, matrix products: 58.2 us -> none  [the longest x8 32.6 us: block_terms(): lax.dot_general(scaled, chosen, (((1, 2), (1, 2)), ((), ())), preferred_e...]
    ppermute x4 -> x0, waiting for transfers between devices: 52.7 us -> none  [the longest x2 52.7 us: extended(): lax.ppermute(lax.slice_in_dim(block, block.shape[dim] - width, None, axis...]
    psum x1 -> x0, waiting for transfers between devices: 45 us -> none  [per_device(): lax.psum((jnp.sum(obs_prior, axis=0, dtype=jnp.float32), jnp.sum(ens_stat...]
    reduce_scatter x2 -> x0, waiting for transfers between devices: 43.9 us -> none  [the longest x1 39 us: per_device(): lax.psum_scatter(jnp.transpose(product, (1, 0, 2)), 'mem', scatter_dimens...]
    all_to_all x1 -> x0, blocking collectives: 30.5 us -> none  [per_device(): lax.all_to_all(perturb, 'mem', split_axis=2, concat_axis=0, tiled=True)]
    while x34 -> x0, local copies, waits for them, and re-layouts: 18.5 us -> none  [the longest x2 14.8 us: run_groups(): result = lax.map(lambda part_items: jax.vmap(func)(*part_items), shaped)]
  transfers between devices with their start and end apart: 8 -> 0, of which waited for: 5 -> 0; matrix products, arithmetic and copies ran while one was open for 2% -> 0% of each run, Pallas kernels for 0% -> 0%
where the time goes in v1:
time: 65.1 us; the launch traced here: 64.9 us
  Pallas kernels  61.8 us (95%)
  local copies, waits for them, and re-layouts  2.19 us (3%)
  other arithmetic  0.89 us (1%)
    pallas_call x1, Pallas kernels, per_device(): pl.pallas_call(functools.partial(kernel, dims), out_shape=jax.ShapeDtypeS...  61.8 us

profile of v1, /device:TPU:0, one launch (start us, length us, event | category | flops | bytes accessed | tf_op | source)
XLA Modules:
  0.0 64.9 jit_solution(14603776530622175692)
XLA Ops:
  0.0 0.0 copy-start.2
  0.0 0.0 copy-start.1
  0.0 0.0 copy-start.3
  0.0 0.0 copy-start.4
  0.0 0.0 copy-start
  0.0 0.8 %convert_element_type.5 = f32[384]{0:T(512)S(1)} convert(s32[384]{0:T(512)} %param.11) | non-fusion elementwise | flops 384 | bytes 3072 | tf_op jit(solution)/shard_map/convert_element_type | solution.py:328
  0.8 0.1 stack_broadcast_in_dim.2
  1.0 1.2 %copy.11 = bf16[20,16,512]{2,0,1:T(8,128)(2,1)S(1)} copy(bf16[20,16,512]{2,1,0:T(8,128)(2,1)} %param.7) | data formatting | bytes 655360 | tf_op args[0]
  2.2 0.0 copy-done.2
  2.2 0.0 copy-done.3
  2.2 0.0 copy-done.4
  2.2 0.1 pad_maximum_fusion.aux_ref
  2.3 0.0 copy-done.1
  2.3 0.0 copy-done
  2.3 61.8 %shard_map.73 = bf16[16,32,512]{2,1,0:T(8,128)(2,1)S(1)} custom-call(bf16[16,32,512]{2,1,0:T(8,128)(2,1)S(1)} %pad.4.ens_ref, bf16[20,384,128]{2,1,0:T(8,128)(2,1)S(1)} %copy-done, f32[4,384,128]{2,1,0:T(8,128)S(1)} %pad_maximum_fusion.aux_ref, s32[16,256]{1,0:T(8,128)S(1)} %copy-done.1), custom_call_target="tpu_custom_call" | custom-call | tf_op jit(solution)/shard_map/pallas_call | solution.py:335
  64.1 0.8 %copy.9 = bf16[20,16,512]{2,1,0:T(8,128)(2,1)} copy(bf16[20,16,512]{2,0,1:T(8,128)(2,1)S(1)} %slice_bitcast_fusion) | data formatting | bytes 655360 | tf_op jit(solution)/shard_map/transpose | solution.py:372
  (2 shorter events, 0.1 us)
Async XLA Ops:
  0.0 2.2 %copy-start.2 = (f32[384,128]{1,0:T(8,128)S(1)}, f32[384,128]{1,0:T(8,128)}, u32[]{:S(2)}) copy-start(f32[384,128]{1,0:T(8,128)} %param.13) | copy-start | bytes 589828
  0.0 2.3 %copy-start.1 = (s32[16,256]{1,0:T(8,128)S(1)}, s32[16,256]{1,0:T(8,128)}, u32[]{:S(2)}) copy-start(s32[16,256]{1,0:T(8,128)} %pair_ref.1) | copy-start | bytes 49156
  0.0 2.2 %copy-start.3 = (f32[384,128]{1,0:T(8,128)S(1)}, f32[384,128]{1,0:T(8,128)}, u32[]{:S(2)}) copy-start(f32[384,128]{1,0:T(8,128)} %param.10) | copy-start | bytes 589828
  0.0 2.2 %copy-start.4 = (f32[384,128]{1,0:T(8,128)S(1)}, f32[384,128]{1,0:T(8,128)}, u32[]{:S(2)}) copy-start(f32[384,128]{1,0:T(8,128)} %param.9) | copy-start | bytes 589828
  0.0 2.3 %copy-start = (bf16[20,384,128]{2,1,0:T(8,128)(2,1)S(1)}, bf16[20,384,128]{2,1,0:T(8,128)(2,1)}, u32[]{:S(2)}) copy-start(bf16[20,384,128]{2,1,0:T(8,128)(2,1)} %obs_ref.1) | copy-start | bytes 5898244
